TPU v7x, 32 devices: a whole 2x2x4 slice. The times are simulated.
32 devices in a mesh: walk: 16 (over z, x, core), elec: 2 (over y).
Axes of the slice: x: 2, y: 2, z: 4, core: 2. Of those that a mesh axis runs over, the one named last changes fastest.
Arguments:
- positions: float32 [96, 3, 200], P('walk', None, 'elec'), may hold values from -5 to 5
- targets: bfloat16 [96, 200, 3200], P('walk', 'elec'), may hold values from -6 to 6
- w_in: float32 [4, 256], replicated, may hold values from -3 to 3
- v_in: float32 [4, 32], replicated, may hold values from -3 to 3
- w_up: float32 [2, 256, 32], replicated, may hold values from -0.375 to 0.375
- w_gate: float32 [2, 32, 32], replicated, may hold values from -1 to 1
- w_mix: float32 [2, 256, 256], replicated, may hold values from -0.375 to 0.375
- w_msg: float32 [2, 32, 256], replicated, may hold values from -1 to 1
- bias: float32 [2, 256], replicated, may hold values from -3 to 3
- w_head: bfloat16 [256, 3200], replicated, may hold values from -0.375 to 0.375
Outputs:
- grad_head: float32 [3200, 256], P('walk')
- grad_in: float32 [4, 256], replicated
- grad_up: float32 [2, 256, 32], replicated
- grad_gate: float32 [2, 32, 32], replicated
- grad_mix: float32 [2, 256, 256], replicated
- grad_msg: float32 [2, 32, 256], replicated
- grad_bias: float32 [2, 256], replicated
All inputs are finite; a program needn't handle non-finite values.
Results may differ from a plain program's by a relative error of at most 0.0003.
Values sent between devices are 32-bit elements; how exact they have to be, the bound alone decides.
A program may use at most 192 MiB of HBM per device.

v0:
```python
import jax
import jax.numpy as jnp
from jax import lax
from jax.sharding import PartitionSpec as P

LAYERS = 2
HI = lax.Precision.HIGHEST


def embed_states(pos_rows, w_in):
    radius = jnp.sqrt(jnp.sum(pos_rows * pos_rows, axis=1) + 1.0)
    feats = jnp.concatenate([pos_rows, radius[:, None, :]], axis=1)
    return jnp.tanh(jnp.einsum("wci,ch->wih", feats, w_in, precision=HI))


def embed_pairs(pos_rows, pos_all, v_in):
    diff = pos_rows[:, :, :, None] - pos_all[:, :, None, :]
    dist = jnp.sqrt(jnp.sum(diff * diff, axis=1) + 1.0)
    feats = jnp.concatenate([diff, dist[:, None]], axis=1)
    return jnp.tanh(jnp.einsum("wcie,cp->wiep", feats, v_in, precision=HI))


def layer_update(h_rows, s_all, pairs, w_mix, w_msg, bias, w_gate):
    gates = jax.nn.sigmoid(jnp.einsum("wiep,pq->wieq", pairs, w_gate, precision=HI))
    message = jnp.einsum("wieq,weq->wiq", gates, s_all, precision=HI) / s_all.shape[1]
    pre = jnp.einsum("wih,hk->wik", h_rows, w_mix, precision=HI)
    pre = pre + jnp.einsum("wiq,qk->wik", message, w_msg, precision=HI) + bias
    return jnp.tanh(pre) + h_rows


def on_device(positions, targets, w_in, v_in, w_up, w_gate, w_mix, w_msg, bias, w_head):
    walkers = positions.shape[0] * lax.axis_size("walk")
    pos_all = lax.all_gather(positions, "elec", axis=2, tiled=True)
    pairs = embed_pairs(positions, pos_all, v_in)
    states, pull_in = jax.vjp(lambda weight: embed_states(positions, weight), w_in)
    saved_states = []
    saved_proj = []
    for layer in range(LAYERS):
        up_now = w_up[layer]
        local_proj = jnp.einsum("wjh,hp->wjp", states, up_now, precision=HI)
        proj = lax.all_gather(local_proj, "elec", axis=1, tiled=True)
        saved_states.append(states)
        saved_proj.append(proj)
        states = layer_update(
            states, proj, pairs, w_mix[layer], w_msg[layer], bias[layer], w_gate[layer]
        )
    last = states.reshape(-1, states.shape[2]).astype(jnp.bfloat16)
    orbitals = jnp.dot(last, w_head, preferred_element_type=jnp.float32)
    flat_targets = targets.reshape(-1, targets.shape[2]).astype(jnp.float32)
    d_orb = (2.0 / walkers * (orbitals - flat_targets)).astype(jnp.bfloat16)
    head_part = lax.psum_scatter(
        lax.dot_general(d_orb, last, (((0,), (0,)), ((), ())), preferred_element_type=jnp.float32),
        "walk",
        scatter_dimension=0,
        tiled=True,
    )
    d_states = lax.dot_general(
        d_orb, w_head, (((1,), (1,)), ((), ())), preferred_element_type=jnp.float32
    )
    d_states = d_states.reshape(states.shape)
    grads_up = [None] * LAYERS
    grads_gate = [None] * LAYERS
    grads_mix = [None] * LAYERS
    grads_msg = [None] * LAYERS
    grads_bias = [None] * LAYERS
    for layer in reversed(range(LAYERS)):

        def local_layer(h_rows, s_all, mix, msg, shift, gate):
            return layer_update(h_rows, s_all, pairs, mix, msg, shift, gate)

        _, pull = jax.vjp(
            local_layer,
            saved_states[layer],
            saved_proj[layer],
            w_mix[layer],
            w_msg[layer],
            bias[layer],
            w_gate[layer],
        )
        d_rows, d_proj, d_mix, d_msg, d_bias, d_gate = pull(d_states)
        d_proj_own = lax.psum_scatter(d_proj, "elec", scatter_dimension=1, tiled=True)
        grads_up[layer] = jnp.einsum("wjh,wjp->hp", saved_states[layer], d_proj_own, precision=HI)
        d_states = d_rows + jnp.einsum("wjp,hp->wjh", d_proj_own, w_up[layer], precision=HI)
        grads_gate[layer] = d_gate
        grads_mix[layer] = d_mix
        grads_msg[layer] = d_msg
        grads_bias[layer] = d_bias
    grad_in = pull_in(d_states)[0]
    grad_up = jnp.stack(grads_up)
    grad_gate = jnp.stack(grads_gate)
    grad_mix = jnp.stack(grads_mix)
    grad_msg = jnp.stack(grads_msg)
    grad_bias = jnp.stack(grads_bias)
    grad_in, grad_up, grad_gate, grad_mix, grad_msg, grad_bias = lax.psum(
        (grad_in, grad_up, grad_gate, grad_mix, grad_msg, grad_bias), ("walk", "elec")
    )
    grad_head = lax.psum(head_part, "elec")
    return (grad_head, grad_in, grad_up, grad_gate, grad_mix, grad_msg, grad_bias)


def solution(mesh):
    return jax.shard_map(
        on_device,
        mesh=mesh,
        in_specs=(
            P("walk", None, "elec"),
            P("walk", "elec", None),
            P(),
            P(),
            P(),
            P(),
            P(),
            P(),
            P(),
            P(),
        ),
        out_specs=(P("walk", None), P(), P(), P(), P(), P(), P()),
        check_vma=False,
    )
```

profile of v0, /device:TPU:0, one launch (start us, length us, event | category | flops | bytes accessed | tf_op | source)
XLA Modules:
  0.0 474.8 jit_solution(301974054413448681)
XLA Ops:
  15.3 13.1 %all_gather.13 = f32[6,200,32]{2,0,1:T(8,128)S(1)} all-gather(f32[6,100,32]{2,0,1:T(8,128)S(1)} %copy.41), channel_id=1, replica_groups=mesh['walk'=16,'elec'=2] {'elec'}, dimensions={1}, use_global_device_ids=true | all-gather | bytes 230400 | tf_op jit(solution)/shard_map/all_gather | solution.py:41
  29.3 7.1 %all_gather.14 = f32[6,3,200]{0,1,2:T(4,128)S(1)} all-gather(f32[6,3,100]{0,1,2:T(4,128)} %copy.43), channel_id=1, replica_groups=mesh['walk'=16,'elec'=2] {'elec'}, dimensions={2}, use_global_device_ids=true | all-gather | bytes 21600 | tf_op jit(solution)/shard_map/all_gather | solution.py:33
  36.7 3.9 broadcast_subtract_fusion
  43.3 19.8 %fusion.30 = f32[6,100,200,32]{2,3,1,0:T(8,128)} fusion(f32[6,1,100,200]{3,1,2,0:T(1,128)S(1)} %copy.46, f32[6,3,100,200]{3,1,2,0:T(4,128)} %get-tuple-element.19, f32[4,32]{1,0:T(4,128)} %param.13), kind=kOutput, calls=%fused_computation.31 | convolution fusion | flops 184800000 | bytes 17280512 | tf_op jit(solution)/shard_map/wcie,cp->wiep/dot_general | solution.py:20
  63.1 28.5 %multiply_reduce_fusion.1 = (f32[6,32,100]{1,2,0:T(8,128)S(1)}, f32[6,100,200,32]{2,3,1,0:T(8,128)}) fusion(f32[6,32,200]{2,1,0:T(8,128)S(1)} %copy-done.11, f32[2,32,32]{2,1,0:T(8,128)S(1)} %copy-done.18, f32[6,100,200,32]{2,3,1,0:T(8,128)} %fusion.30), kind=kOutput, calls=%fused_computation.13 | convolution fusion | flops 1493740800 | bytes 31009792 | tf_op jit(solution)/shard_map/wiep,pq->wieq/dot_general | solution.py:24
  96.5 14.7 %all_gather.15 = f32[6,200,32]{2,0,1:T(8,128)} all-gather(f32[6,100,32]{2,0,1:T(8,128)} %copy.48), channel_id=1, replica_groups=mesh['walk'=16,'elec'=2] {'elec'}, dimensions={1}, use_global_device_ids=true | all-gather | bytes 230400 | tf_op jit(solution)/shard_map/all_gather | solution.py:41
  111.2 2.1 copy.88
  113.2 28.6 %multiply_reduce_fusion = (f32[6,32,100]{1,2,0:T(8,128)}, f32[6,100,200,32]{2,3,1,0:T(8,128)}) fusion(f32[6,32,200]{2,1,0:T(8,128)} %copy.88, f32[2,32,32]{2,1,0:T(8,128)} %param.15, f32[6,100,200,32]{2,3,1,0:T(8,128)} %fusion.30), kind=kOutput, calls=%fused_computation.12 | convolution fusion | flops 1493740800 | bytes 35310592 | tf_op jit(solution)/shard_map/wiep,pq->wieq/dot_general | solution.py:24
  144.4 1.6 add_convert_fusion
  147.1 5.9 %reshape.61 = f32[600,3200]{1,0:T(8,128)} reshape(bf16[6,100,3200]{2,1,0:T(8,128)(2,1)} %param.11) | data formatting | bytes 11520000 | tf_op jit(solution)/shard_map/convert_element_type | solution.py:49
  153.0 4.4 multiply_convert_fusion
  157.4 1.8 copy-done.1
  159.2 2.1 fusion.117
  161.3 2.0 reshape.60
  163.3 1.9 fusion.113
  167.4 26.3 %fusion.2 = f32[6,32,1,200]{3,2,1,0:T(1,128)S(1)} fusion(f32[6,32,100,1]{2,3,1,0:T(1,128)S(1)} %bitcast.196, f32[6,100,200,32]{2,3,1,0:T(8,128)} %get-tuple-element.28), kind=kOutput, calls=%fused_computation.4 | convolution fusion | flops 46080000 | bytes 15590400 | tf_op jit(solution)/shard_map/transpose(jvp(wieq,weq->wiq))/dot_general | solution.py:25
  194.7 5.3 %fusion.116 = f32[3200,256]{1,0:T(8,128)} fusion(bf16[600,3200]{1,0:T(8,128)(2,1)} %copy-done.1, bf16[600,256]{1,0:T(8,128)(2,1)} %copy-done.3), kind=kOutput, calls=%fused_computation.141 | convolution fusion | flops 983040000 | bytes 7424000 | tf_op jit(solution)/shard_map/dot_general | solution.py:52
  200.1 2.0 convolution_bitcast_fusion
  202.1 1.8 copy.52
  203.8 24.5 %fusion.39 = f32[1,32,32]{2,1,0:T(8,128)} fusion(f32[6,100,200,32]{2,3,1,0:T(8,128)} %get-tuple-element.28, f32[6,32,200]{2,1,0:T(8,128)} %copy.88, f32[6,32,100]{1,2,0:T(8,128)} %copy.52, f32[6,100,200,32]{2,3,1,0:T(8,128)} %fusion.30), kind=kOutput, calls=%fused_computation.57 | convolution fusion | flops 1489920000 | bytes 30954496 | tf_op jit(solution)/shard_map/transpose(jvp(wiep,pq->wieq))/dot_general | solution.py:24
  231.4 2.7 convolution_add_fusion.1
  234.1 3.7 fusion.112
  240.0 26.7 %fusion = f32[6,32,1,200]{3,2,1,0:T(1,128)S(1)} fusion(f32[6,32,100,1]{2,3,1,0:T(1,128)S(1)} %bitcast.198, f32[6,100,200,32]{2,3,1,0:T(8,128)} %get-tuple-element.24), kind=kOutput, calls=%fused_computation.2 | convolution fusion | flops 46080000 | bytes 15590400 | tf_op jit(solution)/shard_map/transpose(jvp(wieq,weq->wiq))/dot_general | solution.py:25
  267.3 1.8 copy.50
  269.1 24.1 %fusion.44 = f32[1,32,32]{2,1,0:T(8,128)S(1)} fusion(f32[6,100,200,32]{2,3,1,0:T(8,128)} %get-tuple-element.24, f32[6,32,200]{2,1,0:T(8,128)} %copy.87, f32[6,32,100]{1,2,0:T(8,128)} %copy.50, f32[6,100,200,32]{2,3,1,0:T(8,128)} %fusion.30), kind=kOutput, calls=%fused_computation.58 | convolution fusion | flops 1489920000 | bytes 30954496 | tf_op jit(solution)/shard_map/transpose(jvp(wiep,pq->wieq))/dot_general | solution.py:24
  299.6 1.9 convolution_add_fusion
  301.5 23.3 %all-reduce.13.cloned.1.call-done = (f32[200,256]{1,0:T(8,128)}, f32[6,200,32]{1,2,0:T(8,128)}) async-done(((f32[200,256]{1,0:T(8,128)}, f32[6,200,32]{1,2,0:T(8,128)}), (f32[200,256]{1,0:T(8,128)}, f32[6,200,32]{1,2,0:T(8,128)})) %all-reduce.13.cloned.1.call-update) | async-done | bytes 358416 | tf_op jit(solution)/shard_map/psum | solution.py:97
  327.7 1.8 fusion.34
  330.6 40.5 %all-reduce.2 = (f32[4,256]{1,0:T(4,128)}, f32[2,32,32]{2,1,0:T(8,128)}, f32[2,256]{1,0:T(2,128)}) all-reduce(f32[4,256]{1,0:T(4,128)S(1)} %convolution_bitcast_fusion.6, f32[2,32,32]{2,1,0:T(8,128)} %pad_maximum_fusion.3, f32[2,256]{1,0:T(2,128)} %pad_maximum_fusion.7), channel_id=1, replica_groups=mesh['walk'=16,'elec'=2] {'walk','elec'}, use_global_device_ids=true, to_apply=%region_6.0 | all-reduce | flops 3584 | bytes 28672 | tf_op jit(solution)/shard_map/psum | solution.py:94
  371.0 89.6 %all-reduce.11.cloned.1.call-done = (f32[2,256,32]{1,2,0:T(8,128)}, f32[2,256,256]{2,1,0:T(8,128)}, f32[2,32,256]{2,1,0:T(8,128)}) async-done(((f32[2,256,32]{1,2,0:T(8,128)}, f32[2,256,256]{2,1,0:T(8,128)}, f32[2,32,256]{2,1,0:T(8,128)}), (f32[2,256,32]{1,2,0:T(8,128)}, f32[2,256,256]{2,1,0:T(8,128)}, f32[2,32,256]{2,1,0:T(8,128)})) %all-reduce.11.cloned.1.call-update) | async-done | bytes 655376 | tf_op jit(solution)/shard_map/psum | solution.py:94
  460.7 1.6 copy.105
  463.8 1.9 copy.107
  (87 shorter events, 41.2 us)
Async XLA Ops:
  8.0 145.0 %copy-start = (bf16[256,3200]{1,0:T(8,128)(2,1)S(1)}, bf16[256,3200]{1,0:T(8,128)(2,1)}, u32[]{:S(2)}) copy-start(bf16[256,3200]{1,0:T(8,128)(2,1)} %param.19) | copy-start | bytes 4915204
  8.0 226.1 %all-reduce.9.cloned.1.call-start = ((), (), s32[]{:S(2)}) async-start(), calls=%async_computation.2 | async-start | bytes 393216
  12.1 1.5 copy-start.16
  41.9 21.2 %copy-start.18 = (f32[2,32,32]{2,1,0:T(8,128)S(1)}, f32[2,32,32]{2,1,0:T(8,128)}, u32[]{:S(2)}) copy-start(f32[2,32,32]{2,1,0:T(8,128)} %param.15) | copy-start | bytes 24580
  43.3 19.8 %copy-start.11 = (f32[6,32,200]{2,1,0:T(8,128)S(1)}, f32[6,32,200]{2,1,0:T(8,128)}, u32[]{:S(2)}) copy-start(f32[6,32,200]{2,1,0:T(8,128)} %copy.87) | copy-start | bytes 460804
  63.1 28.6 %copy-start.17 = (f32[2,256]{1,0:T(2,128)S(1)}, f32[2,256]{1,0:T(2,128)}, u32[]{:S(2)}) copy-start(f32[2,256]{1,0:T(2,128)} %param.18) | copy-start | bytes 6148
  63.1 28.6 %copy-start.12 = (f32[2,32,256]{2,1,0:T(8,128)S(1)}, f32[2,32,256]{2,1,0:T(8,128)}, u32[]{:S(2)}) copy-start(f32[2,32,256]{2,1,0:T(8,128)} %param.17) | copy-start | bytes 196612
  63.1 29.3 %copy-start.2 = (f32[2,256,256]{2,1,0:T(8,128)S(1)}, f32[2,256,256]{2,1,0:T(8,128)}, u32[]{:S(2)}) copy-start(f32[2,256,256]{2,1,0:T(8,128)} %param.16) | copy-start | bytes 1572868
  91.7 0.7 copy-start.7
  142.9 20.4 %copy-start.9 = (f32[6,32,100]{2,1,0:T(8,128)}, f32[6,32,100]{2,1,0:T(8,128)S(1)}, u32[]{:S(2)}) copy-start(f32[6,32,100]{2,1,0:T(8,128)S(1)} %copy.72) | copy-start | bytes 230404
  147.1 16.2 %copy-start.3 = (bf16[600,256]{1,0:T(8,128)(2,1)}, bf16[600,256]{1,0:T(8,128)(2,1)S(1)}, u32[]{:S(2)}) copy-start(bf16[600,256]{1,0:T(8,128)(2,1)S(1)} %convert_element_type.16) | copy-start | bytes 921604
  157.4 1.8 copy-start.1
  166.8 0.7 copy-start.4
  194.4 103.8 %reduce-scatter.4.cloned.1.call-start = ((), (), s32[]{:S(2)}) async-start(), calls=%async_computation.1 | async-start | bytes 3481600 | tf_op jit(solution)/shard_map/reduce_scatter | solution.py:51
  200.0 124.7 %all-reduce.13.cloned.1.call-start = ((), (), s32[]{:S(2)}) async-start(), calls=%async_computation.4 | async-start | bytes 802816 | tf_op jit(solution)/shard_map/psum | solution.py:97
  203.8 24.5 %copy-start.10 = (f32[6,32,100]{2,1,0:T(8,128)S(1)}, f32[6,32,100]{2,1,0:T(8,128)}, u32[]{:S(2)}) copy-start(f32[6,32,100]{2,1,0:T(8,128)} %copy-done.9) | copy-start | bytes 230404
  239.3 0.6 copy-start.5
  269.1 24.1 %copy-start.15 = (f32[1,32,32]{2,1,0:T(8,128)S(1)}, f32[1,32,32]{2,1,0:T(8,128)}, u32[]{:S(2)}) copy-start(f32[1,32,32]{2,1,0:T(8,128)} %fusion.39) | copy-start | bytes 12292
  269.1 24.7 %copy-start.8 = (f32[6,32,100]{2,1,0:T(8,128)S(1)}, f32[6,32,100]{2,1,0:T(8,128)}, u32[]{:S(2)}) copy-start(f32[6,32,100]{2,1,0:T(8,128)} %copy-done.7) | copy-start | bytes 230404
  269.1 25.2 %copy-start.14 = (f32[1,32,256]{2,1,0:T(8,128)S(1)}, f32[1,32,256]{2,1,0:T(8,128)}, u32[]{:S(2)}) copy-start(f32[1,32,256]{2,1,0:T(8,128)} %convolution_bitcast_fusion.2) | copy-start | bytes 98308
  269.1 27.1 %copy-start.6 = (f32[1,256,256]{2,1,0:T(8,128)S(1)}, f32[1,256,256]{2,1,0:T(8,128)}, u32[]{:S(2)}) copy-start(f32[1,256,256]{2,1,0:T(8,128)} %convolution_bitcast_fusion) | copy-start | bytes 786436
  269.1 28.0 %copy-start.13 = (f32[6,200,32]{1,2,0:T(8,128)S(1)}, f32[6,200,32]{1,2,0:T(8,128)}, u32[]{:S(2)}) copy-start(f32[6,200,32]{1,2,0:T(8,128)} %all-reduce.9.cloned.1.call-done) | copy-start | bytes 460804
  298.3 162.4 %all-reduce.11.cloned.1.call-start = ((), (), s32[]{:S(2)}) async-start(), calls=%async_computation.3 | async-start | bytes 1310720 | tf_op jit(solution)/shard_map/psum | solution.py:94
Sparse Core Ops, SparseCore 0:
  194.6 22.5 all-reduce.8
  298.4 26.2 all-reduce.12
  330.9 129.7 all-reduce.10
Sparse Core Ops, SparseCore 1:
  200.1 67.0 reduce-scatter.3
where the time goes:
time: 483 us; the launch traced here: 475 us
  matrix products  222 us (46%)
  waiting for transfers between devices  113 us (23%)
  blocking collectives  75.4 us (16%)
  local copies, waits for them, and re-layouts  35.1 us (7%)
  between operations  16.7 us (3%)
  other arithmetic  12.4 us (3%)
    dot_general x4, matrix products, layer_update(): jnp.einsum('wiep,pq->wieq', pairs, w_gate, precision=HI)  106 us
    psum x1, waiting for transfers between devices, on_device(): lax.psum((grad_in, grad_up, grad_gate, grad_mix, grad_msg, grad_bias), ('...  89.6 us
    dot_general x2, matrix products, layer_update(): jnp.einsum('wieq,weq->wiq', gates, s_all, precision=HI) / s_all.shape[1]  53 us
    psum x1, blocking collectives, on_device(): lax.psum((grad_in, grad_up, grad_gate, grad_mix, grad_msg, grad_bias), ('...  40.5 us
    all_gather x2, blocking collectives, on_device(): proj = lax.all_gather(local_proj, 'elec', axis=1, tiled=True)  27.8 us
    psum x1, waiting for transfers between devices, on_device(): grad_head = lax.psum(head_part, 'elec')  23.3 us
    dot_general x1, matrix products, embed_pairs(): return jnp.tanh(jnp.einsum('wcie,cp->wiep', feats, v_in, precision=HI))  19.8 us
    unnamed x47, local copies, waits for them, and re-layouts  17 us
  transfers between devices with their start and end apart: 4, of which 2 were waited for; matrix products, arithmetic and copies ran while one was open for 23% of the time, Pallas kernels for 0%

commit v1 on v0

--- a/solution.py
+++ b/solution.py
@@ -94,7 +94,7 @@
     grad_in, grad_up, grad_gate, grad_mix, grad_msg, grad_bias = lax.psum(
         (grad_in, grad_up, grad_gate, grad_mix, grad_msg, grad_bias), ("walk", "elec")
     )
-    grad_head = lax.psum(head_part, "elec")
+    grad_head = jnp.sum(lax.all_gather(head_part, "elec"), axis=0)
     return (grad_head, grad_in, grad_up, grad_gate, grad_mix, grad_msg, grad_bias)
 
 

time: 483 us -> 469 us (0.971)
  waiting for transfers between devices: 113 us -> 97 us
  blocking collectives: 75.4 us -> 82.9 us
    psum x1 -> x0, waiting for transfers between devices: 23.3 us -> none  [on_device(): grad_head = lax.psum(head_part, 'elec')]
    unnamed x5 -> x6, waiting for transfers between devices: 0.07 us -> 18 us
    psum x1, waiting for transfers between devices: 89.6 us -> 79 us  [on_device(): lax.psum((grad_in, grad_up, grad_gate, grad_mix, grad_msg, grad_bias), ('...]
    all_gather x0 -> x1, blocking collectives: none -> 7.29 us  [on_device(): grad_head = jnp.sum(lax.all_gather(head_part, 'elec'), axis=0)]
    unnamed x47 -> x60, local copies, waits for them, and re-layouts: 17 us -> 16.3 us
  transfers between devices with their start and end apart: 4 -> 4, of which waited for: 2 -> 2; matrix products, arithmetic and copies ran while one was open for 23% -> 16% of each run, Pallas kernels for 0% -> 0%
where the time goes in v1:
time: 469 us; the launch traced here: 461 us
  matrix products  218 us (46%)
  waiting for transfers between devices  97 us (21%)
  blocking collectives  82.9 us (18%)
  local copies, waits for them, and re-layouts  33.7 us (7%)
  between operations  16.8 us (4%)
  other arithmetic  11.2 us (2%)
    dot_general x4, matrix products, layer_update(): jnp.einsum('wiep,pq->wieq', pairs, w_gate, precision=HI)  105 us
    psum x1, waiting for transfers between devices, on_device(): lax.psum((grad_in, grad_up, grad_gate, grad_mix, grad_msg, grad_bias), ('...  79 us
    dot_general x2, matrix products, layer_update(): jnp.einsum('wieq,weq->wiq', gates, s_all, precision=HI) / s_all.shape[1]  52.6 us
    psum x1, blocking collectives, on_device(): lax.psum((grad_in, grad_up, grad_gate, grad_mix, grad_msg, grad_bias), ('...  40.6 us
    all_gather x2, blocking collectives, on_device(): proj = lax.all_gather(local_proj, 'elec', axis=1, tiled=True)  27.8 us
    dot_general x1, matrix products, embed_pairs(): return jnp.tanh(jnp.einsum('wcie,cp->wiep', feats, v_in, precision=HI))  19.8 us
    unnamed x6, waiting for transfers between devices  18 us
    unnamed x60, local copies, waits for them, and re-layouts  16.3 us
  transfers between devices with their start and end apart: 4, of which 2 were waited for; matrix products, arithmetic and copies ran while one was open for 16% of the time, Pallas kernels for 0%

profile of v1, /device:TPU:0, one launch (start us, length us, event | category | flops | bytes accessed | tf_op | source)
XLA Modules:
  0.0 460.6 jit_solution(8299413091901412185)
XLA Ops:
  8.9 1.5 copy.43
  10.4 1.6 copy.42
  15.3 13.1 %all_gather.19 = f32[6,200,32]{2,0,1:T(8,128)S(1)} all-gather(f32[6,100,32]{2,0,1:T(8,128)S(1)} %copy.41), channel_id=1, replica_groups=mesh['walk'=16,'elec'=2] {'elec'}, dimensions={1}, use_global_device_ids=true | all-gather | bytes 230400 | tf_op jit(solution)/shard_map/all_gather | solution.py:41
  29.3 7.1 %all_gather.20 = f32[6,3,200]{0,1,2:T(4,128)S(1)} all-gather(f32[6,3,100]{0,1,2:T(4,128)} %copy.43), channel_id=1, replica_groups=mesh['walk'=16,'elec'=2] {'elec'}, dimensions={2}, use_global_device_ids=true | all-gather | bytes 21600 | tf_op jit(solution)/shard_map/all_gather | solution.py:33
  36.7 3.9 broadcast_subtract_fusion
  43.3 19.8 %fusion.30 = f32[6,100,200,32]{2,3,1,0:T(8,128)} fusion(f32[6,1,100,200]{3,1,2,0:T(1,128)S(1)} %copy.46, f32[6,3,100,200]{3,1,2,0:T(4,128)} %get-tuple-element.17, f32[4,32]{1,0:T(4,128)} %param.13), kind=kOutput, calls=%fused_computation.31 | convolution fusion | flops 184800000 | bytes 17280512 | tf_op jit(solution)/shard_map/wcie,cp->wiep/dot_general | solution.py:20
  63.1 28.5 %multiply_reduce_fusion.1 = (f32[6,32,100]{1,2,0:T(8,128)S(1)}, f32[6,100,200,32]{2,3,1,0:T(8,128)}) fusion(f32[6,32,200]{2,1,0:T(8,128)S(1)} %copy-done.15, f32[2,32,32]{2,1,0:T(8,128)S(1)} %copy-done.25, f32[6,100,200,32]{2,3,1,0:T(8,128)} %fusion.30), kind=kOutput, calls=%fused_computation.13 | convolution fusion | flops 1493740800 | bytes 31009792 | tf_op jit(solution)/shard_map/wiep,pq->wieq/dot_general | solution.py:24
  96.5 14.7 %all_gather.21 = f32[6,200,32]{2,0,1:T(8,128)} all-gather(f32[6,100,32]{2,0,1:T(8,128)} %copy.48), channel_id=1, replica_groups=mesh['walk'=16,'elec'=2] {'elec'}, dimensions={1}, use_global_device_ids=true | all-gather | bytes 230400 | tf_op jit(solution)/shard_map/all_gather | solution.py:41
  111.2 2.1 copy.88
  113.3 28.6 %multiply_reduce_fusion = (f32[6,32,100]{1,2,0:T(8,128)}, f32[6,100,200,32]{2,3,1,0:T(8,128)}) fusion(f32[6,32,200]{2,1,0:T(8,128)} %copy.88, f32[2,32,32]{2,1,0:T(8,128)} %param.15, f32[6,100,200,32]{2,3,1,0:T(8,128)} %fusion.30), kind=kOutput, calls=%fused_computation.12 | convolution fusion | flops 1493740800 | bytes 35310592 | tf_op jit(solution)/shard_map/wiep,pq->wieq/dot_general | solution.py:24
  144.5 1.6 add_convert_fusion
  147.1 5.9 %reshape.61 = f32[600,3200]{1,0:T(8,128)} reshape(bf16[6,100,3200]{2,1,0:T(8,128)(2,1)} %param.11) | data formatting | bytes 11520000 | tf_op jit(solution)/shard_map/convert_element_type | solution.py:49
  153.0 4.4 multiply_convert_fusion
  157.4 1.8 copy-done.3
  159.3 2.1 fusion.117
  161.4 2.0 reshape.60
  163.3 2.0 fusion.113
  167.5 26.3 %fusion.2 = f32[6,32,1,200]{3,2,1,0:T(1,128)S(1)} fusion(f32[6,32,100,1]{2,3,1,0:T(1,128)S(1)} %bitcast.198, f32[6,100,200,32]{2,3,1,0:T(8,128)} %get-tuple-element.26), kind=kOutput, calls=%fused_computation.4 | convolution fusion | flops 46080000 | bytes 15590400 | tf_op jit(solution)/shard_map/transpose(jvp(wieq,weq->wiq))/dot_general | solution.py:25
  196.7 2.7 convolution_add_fusion.1
  199.4 17.9 %all-reduce.8.cloned.1.call-done = f32[6,200,32]{1,2,0:T(8,128)} async-done(((f32[6,200,32]{1,2,0:T(8,128)}), f32[6,200,32]{1,2,0:T(8,128)}) %all-reduce.8.cloned.1.call-update) | async-done | bytes 153616
  217.3 3.7 fusion.112
  224.0 26.3 %fusion = f32[6,32,1,200]{3,2,1,0:T(1,128)S(1)} fusion(f32[6,32,100,1]{2,3,1,0:T(1,128)S(1)} %bitcast.200, f32[6,100,200,32]{2,3,1,0:T(8,128)} %get-tuple-element.22), kind=kOutput, calls=%fused_computation.2 | convolution fusion | flops 46080000 | bytes 15590400 | tf_op jit(solution)/shard_map/transpose(jvp(wieq,weq->wiq))/dot_general | solution.py:25
  251.1 5.3 %fusion.116 = f32[3200,256]{1,0:T(8,128)} fusion(bf16[600,3200]{1,0:T(8,128)(2,1)} %copy-done.3, bf16[600,256]{1,0:T(8,128)(2,1)} %copy-done.7), kind=kOutput, calls=%fused_computation.141 | convolution fusion | flops 983040000 | bytes 7424000 | tf_op jit(solution)/shard_map/dot_general | solution.py:52
  256.7 1.8 copy.52
  258.5 24.3 %fusion.39 = f32[1,32,32]{2,1,0:T(8,128)} fusion(f32[6,100,200,32]{2,3,1,0:T(8,128)} %get-tuple-element.26, f32[6,32,200]{2,1,0:T(8,128)} %copy.88, f32[6,32,100]{1,2,0:T(8,128)} %copy.52, f32[6,100,200,32]{2,3,1,0:T(8,128)} %fusion.30), kind=kOutput, calls=%fused_computation.57 | convolution fusion | flops 1489920000 | bytes 30954496 | tf_op jit(solution)/shard_map/transpose(jvp(wiep,pq->wieq))/dot_general | solution.py:24
  283.9 2.0 convolution_bitcast_fusion
  287.8 23.8 %fusion.44 = f32[1,32,32]{2,1,0:T(8,128)S(1)} fusion(f32[6,100,200,32]{2,3,1,0:T(8,128)} %get-tuple-element.22, f32[6,32,200]{2,1,0:T(8,128)} %copy.87, f32[6,32,100]{1,2,0:T(8,128)S(1)} %copy.50, f32[6,100,200,32]{2,3,1,0:T(8,128)} %fusion.30), kind=kOutput, calls=%fused_computation.58 | convolution fusion | flops 1489920000 | bytes 30954496 | tf_op jit(solution)/shard_map/transpose(jvp(wiep,pq->wieq))/dot_general | solution.py:24
  318.4 1.8 fusion.34
  320.6 40.6 %all-reduce.2 = (f32[4,256]{1,0:T(4,128)}, f32[2,32,32]{2,1,0:T(8,128)}, f32[2,256]{1,0:T(2,128)}) all-reduce(f32[4,256]{1,0:T(4,128)S(1)} %convolution_bitcast_fusion.6, f32[2,32,32]{2,1,0:T(8,128)S(1)} %pad_maximum_fusion.3, f32[2,256]{1,0:T(2,128)S(1)} %pad_maximum_fusion.7), channel_id=1, replica_groups=mesh['walk'=16,'elec'=2] {'walk','elec'}, use_global_device_ids=true, to_apply=%region_6.0 | all-reduce | flops 3584 | bytes 28672 | tf_op jit(solution)/shard_map/psum | solution.py:94
  361.2 7.3 %all-gather = f32[400,256]{1,0:T(8,128)S(1)} all-gather(f32[200,256]{1,0:T(8,128)} %reduce-scatter.4.cloned.1.call-done), channel_id=2, replica_groups=mesh['walk'=16,'elec'=2] {'elec'}, dimensions={0}, use_global_device_ids=true | all-gather | bytes 614400 | tf_op jit(solution)/shard_map/all_gather | solution.py:97
  369.2 79.0 %all-reduce.12.cloned.1.call-done = (f32[2,256,32]{1,2,0:T(8,128)}, f32[2,256,256]{2,1,0:T(8,128)}, f32[2,32,256]{2,1,0:T(8,128)}) async-done(((f32[2,256,32]{1,2,0:T(8,128)}, f32[2,256,256]{2,1,0:T(8,128)}, f32[2,32,256]{2,1,0:T(8,128)}), (f32[2,256,32]{1,2,0:T(8,128)}, f32[2,256,256]{2,1,0:T(8,128)}, f32[2,32,256]{2,1,0:T(8,128)})) %all-reduce.12.cloned.1.call-update) | async-done | bytes 655376 | tf_op jit(solution)/shard_map/psum | solution.py:94
  449.7 1.9 copy.105
  (102 shorter events, 38.4 us)
Async XLA Ops:
  8.0 145.0 %copy-start = (bf16[256,3200]{1,0:T(8,128)(2,1)S(1)}, bf16[256,3200]{1,0:T(8,128)(2,1)}, u32[]{:S(2)}) copy-start(bf16[256,3200]{1,0:T(8,128)(2,1)} %param.19) | copy-start | bytes 4915204
  8.0 209.2 %all-reduce.8.cloned.1.call-start = ((), (), s32[]{:S(2)}) async-start(), calls=%async_computation.2 | async-start | bytes 393216
  12.1 1.5 copy-start.22
  41.9 21.2 %copy-start.25 = (f32[2,32,32]{2,1,0:T(8,128)S(1)}, f32[2,32,32]{2,1,0:T(8,128)}, u32[]{:S(2)}) copy-start(f32[2,32,32]{2,1,0:T(8,128)} %param.15) | copy-start | bytes 24580
  43.3 19.8 %copy-start.15 = (f32[6,32,200]{2,1,0:T(8,128)S(1)}, f32[6,32,200]{2,1,0:T(8,128)}, u32[]{:S(2)}) copy-start(f32[6,32,200]{2,1,0:T(8,128)} %copy.87) | copy-start | bytes 460804
  63.1 28.6 %copy-start.24 = (f32[2,256]{1,0:T(2,128)S(1)}, f32[2,256]{1,0:T(2,128)}, u32[]{:S(2)}) copy-start(f32[2,256]{1,0:T(2,128)} %param.18) | copy-start | bytes 6148
  63.1 28.6 %copy-start.18 = (f32[2,32,256]{2,1,0:T(8,128)S(1)}, f32[2,32,256]{2,1,0:T(8,128)}, u32[]{:S(2)}) copy-start(f32[2,32,256]{2,1,0:T(8,128)} %param.17) | copy-start | bytes 196612
  63.1 29.4 %copy-start.5 = (f32[2,256,256]{2,1,0:T(8,128)S(1)}, f32[2,256,256]{2,1,0:T(8,128)}, u32[]{:S(2)}) copy-start(f32[2,256,256]{2,1,0:T(8,128)} %param.16) | copy-start | bytes 1572868
  91.7 0.7 copy-start.11
  143.0 20.4 %copy-start.13 = (f32[6,32,100]{2,1,0:T(8,128)}, f32[6,32,100]{2,1,0:T(8,128)S(1)}, u32[]{:S(2)}) copy-start(f32[6,32,100]{2,1,0:T(8,128)S(1)} %copy.72) | copy-start | bytes 230404
  147.1 16.2 %copy-start.7 = (bf16[600,256]{1,0:T(8,128)(2,1)}, bf16[600,256]{1,0:T(8,128)(2,1)S(1)}, u32[]{:S(2)}) copy-start(bf16[600,256]{1,0:T(8,128)(2,1)S(1)} %convert_element_type.16) | copy-start | bytes 921604
  157.4 1.8 copy-start.3
  166.8 0.6 copy-start.8
  194.5 121.7 %all-reduce.10.cloned.1.call-start = ((), (), s32[]{:S(2)}) async-start(), calls=%async_computation.3 | async-start | bytes 393216
  221.0 0.9 copy-start.1
  223.3 0.6 copy-start.9
  251.0 110.2 %reduce-scatter.4.cloned.1.call-start = ((), (), s32[]{:S(2)}) async-start(), calls=%async_computation.1 | async-start | bytes 3481600 | tf_op jit(solution)/shard_map/reduce_scatter | solution.py:51
  256.4 191.9 %all-reduce.12.cloned.1.call-start = ((), (), s32[]{:S(2)}) async-start(), calls=%async_computation.4 | async-start | bytes 1310720 | tf_op jit(solution)/shard_map/psum | solution.py:94
  258.5 24.3 %copy-start.14 = (f32[6,32,100]{2,1,0:T(8,128)S(1)}, f32[6,32,100]{2,1,0:T(8,128)}, u32[]{:S(2)}) copy-start(f32[6,32,100]{2,1,0:T(8,128)} %copy-done.13) | copy-start | bytes 230404
  287.7 23.9 %copy-start.21 = (f32[1,32,32]{2,1,0:T(8,128)S(1)}, f32[1,32,32]{2,1,0:T(8,128)}, u32[]{:S(2)}) copy-start(f32[1,32,32]{2,1,0:T(8,128)} %fusion.39) | copy-start | bytes 12292
  287.7 24.0 %copy-start.2 = (f32[6,100,256]{2,1,0:T(8,128)S(1)}, f32[6,100,256]{2,1,0:T(8,128)}, u32[]{:S(2)}) copy-start(f32[6,100,256]{2,1,0:T(8,128)} %copy-done.1) | copy-start | bytes 1843204
  287.7 24.0 %copy-start.12 = (f32[6,32,100]{2,1,0:T(8,128)S(1)}, f32[6,32,100]{2,1,0:T(8,128)}, u32[]{:S(2)}) copy-start(f32[6,32,100]{2,1,0:T(8,128)} %copy-done.11) | copy-start | bytes 230404
  287.7 24.5 %copy-start.20 = (f32[1,32,256]{2,1,0:T(8,128)S(1)}, f32[1,32,256]{2,1,0:T(8,128)}, u32[]{:S(2)}) copy-start(f32[1,32,256]{2,1,0:T(8,128)} %convolution_bitcast_fusion.2) | copy-start | bytes 98308
  287.7 26.4 %copy-start.10 = (f32[1,256,256]{2,1,0:T(8,128)S(1)}, f32[1,256,256]{2,1,0:T(8,128)}, u32[]{:S(2)}) copy-start(f32[1,256,256]{2,1,0:T(8,128)} %convolution_bitcast_fusion) | copy-start | bytes 786436
  287.7 27.2 %copy-start.19 = (f32[6,200,32]{1,2,0:T(8,128)S(1)}, f32[6,200,32]{1,2,0:T(8,128)}, u32[]{:S(2)}) copy-start(f32[6,200,32]{1,2,0:T(8,128)} %all-reduce.8.cloned.1.call-done) | copy-start | bytes 460804
  287.7 27.7 %copy-start.4 = (f32[6,100,256]{2,1,0:T(8,128)S(1)}, f32[6,100,256]{2,1,0:T(8,128)}, u32[]{:S(2)}) copy-start(f32[6,100,256]{2,1,0:T(8,128)} %get-tuple-element.29) | copy-start | bytes 1843204
  287.7 27.7 %copy-start.6 = (f32[2,256,256]{2,1,0:T(8,128)S(1)}, f32[2,256,256]{2,1,0:T(8,128)}, u32[]{:S(2)}) copy-start(f32[2,256,256]{2,1,0:T(8,128)} %param.16) | copy-start | bytes 1572868
  287.7 30.6 %copy-start.17 = (f32[2,256,32]{1,2,0:T(8,128)S(1)}, f32[2,256,32]{1,2,0:T(8,128)}, u32[]{:S(2)}) copy-start(f32[2,256,32]{1,2,0:T(8,128)} %param.14) | copy-start | bytes 196612
  287.7 32.5 %copy-start.16 = (f32[6,3,100]{2,1,0:T(4,128)S(1)}, f32[6,3,100]{2,1,0:T(4,128)}, u32[]{:S(2)}) copy-start(f32[6,3,100]{2,1,0:T(4,128)} %param.10) | copy-start | bytes 21604
  287.8 32.5 %copy-start.23 = (f32[6,1,100]{2,1,0:T(1,128)S(1)}, f32[6,1,100]{2,1,0:T(1,128)}, u32[]{:S(2)}) copy-start(f32[6,1,100]{2,1,0:T(1,128)} %copy-done.22) | copy-start | bytes 7204
Sparse Core Ops, SparseCore 0:
  194.6 22.6 all-reduce.7
  251.1 22.3 all-reduce.9
  318.5 129.7 all-reduce.11
Sparse Core Ops, SparseCore 1:
  256.5 66.7 reduce-scatter.3
